TPU v7x, 128 devices: a whole 4x4x4 slice. The times are simulated.
128 devices in a mesh: coil: 4 (over z), slab: 32 (over y, x, core).
Axes of the slice: x: 4, y: 4, z: 4, core: 2. Of those that a mesh axis runs over, the one named last changes fastest.
Arguments:
- image: float32 [2, 256, 256, 256], P(None, 'slab'), may hold values from -6 to 6
- sens: float32 [4, 2, 256, 256, 256], P('coil', None, 'slab'), may hold values from -6 to 6
- weights: bfloat16 [8192, 128, 128], P('slab'), may hold values from -0.5 to 0.5
- bins: int32 [8192], P('slab'), may hold values from 0 to 4095
- counts: int32 [32], P('slab'), may hold values from 32 to 256, as said below
Outputs:
- result: float32 [2, 256, 256, 256], P(None, 'slab', 'coil')
Inputs may be any that keep to these rules, and one draw needn't show every extreme that they name: The two slabs at the middle of the second dimension hold 256 live tiles; counts fall towards the edges of k-space.
All inputs are finite; a program needn't handle non-finite values.
Results may differ from a plain program's by a relative error of at most 0.0003.
Values sent between devices are 32-bit elements; how exact they have to be, the bound alone decides.
A program may use at most 128 MiB of HBM per device.

v0:
```python
import functools

import numpy as np
import jax
import jax.numpy as jnp
import ml_dtypes
from jax import lax
from jax.experimental import pallas as pl
from jax.experimental.pallas import tpu as pltpu
from jax.sharding import PartitionSpec as P

N = 256
TILE = 128
SLOTS = 256
CHIPS = 16
RING = 4
PLANES = 8
GROUPS = 2
SPAN = SLOTS // GROUPS
VMEM_LIMIT = 60 * 1024 * 1024
F32 = jnp.float32
BF16 = jnp.bfloat16


def halves(values):
    high = values.astype(ml_dtypes.bfloat16)
    low = (values - high.astype(np.float64)).astype(ml_dtypes.bfloat16)
    return high, low


def stack(table, axis):
    high, low = halves(table)
    return np.concatenate([high, low, high], axis)


def wave(rows, columns):
    angle = 2.0 * np.pi * (rows[:, None] * columns[None, :] % N) / N
    return np.cos(angle) / 16.0, np.sin(angle) / 16.0


EVEN = 2 * np.arange(TILE)
ODD = (2 * np.arange(TILE) + 1 + TILE) % N


def tables():
    first = np.arange(TILE)
    fwd_right, fwd_left, back_left, back_right = [], [], [], []
    packed = np.arange(2 * TILE).reshape(2, PLANES, 2, 8).transpose(2, 1, 0, 3).reshape(-1)
    for odd in range(2):
        cosine, sine = wave(first, (EVEN, ODD)[odd])
        fwd_right.append(stack(np.block([[cosine, -sine], [sine, cosine]]), 0))
        cosine, sine = wave((EVEN, ODD)[odd], first)
        back_right.append(stack(np.block([[cosine, sine], [-sine, cosine]]), 0))
        cosine, sine = wave(first, 2 * first + odd)
        fwd_left.append(stack(np.block([[cosine, sine], [-sine, cosine]]), 1))
        cosine, sine = wave(2 * first + odd, first)
        back_left.append(stack(np.block([[cosine, -sine], [sine, cosine]])[:, packed], 1))
    lanes = []
    cosine, sine = wave(np.arange(N), np.arange(N))
    for chip in range(CHIPS):
        cos_x = np.repeat(cosine[:, chip * 16 : chip * 16 + 16], 8, axis=1)
        sin_x = np.repeat(sine[:, chip * 16 : chip * 16 + 16], 8, axis=1)
        cos_parts, sin_parts = halves(cos_x), halves(sin_x)
        lanes.append(np.concatenate([cos_parts[0], sin_parts[0], cos_parts[1], sin_parts[1]], 1))
    phases = np.stack(lanes)
    lane = np.arange(TILE)
    order = np.stack([np.where(lane < 64, 2 * lane, 2 * lane - TILE + 1), np.where(lane < 64, 2 * lane + 1, 2 * lane - TILE)])
    natural = np.concatenate([np.eye(TILE)[order[0]], np.eye(TILE)[order[1]]], 0).astype(ml_dtypes.bfloat16)
    return {
        "fwd_right": np.stack(fwd_right),
        "fwd_left": np.stack(fwd_left),
        "back_left": np.stack(back_left),
        "back_right": np.stack(back_right),
        "phases": phases,
        "phases_t": np.ascontiguousarray(phases.transpose(0, 2, 1)),
        "natural": natural,
        "packed": np.ascontiguousarray(natural.T),
    }


def split(values):
    high = values.astype(BF16)
    low = (values - high.astype(F32)).astype(BF16)
    return high, low


def dot(a, b):
    return lax.dot_general(a, b, (((1,), (0,)), ((), ())), preferred_element_type=F32)


def wide(values):
    high, low = split(values)
    return jnp.concatenate([high, high, low], 1)


def tall(values):
    high, low = split(values)
    return jnp.concatenate([high, high, low], 0)


def place():
    slab = lax.axis_index("slab")
    core = lax.rem(slab, 2)
    chip = slab // 2
    x, y = lax.rem(chip, RING), chip // RING
    return core, chip, x, y


def device(x, y, core):
    return {"slab": (y * RING + x) * 2 + core}


def up(i, step=1):
    return lax.rem(i + step, RING)


def down(i):
    return lax.rem(i + RING - 1, RING)


def halved(source, target, sem, i, first):
    return [
        pltpu.make_async_copy(source.at[:, i, :, pl.ds(half * TILE, TILE)], target.at[:, i, half], sem.at[i, first + half])
        for half in range(2)
    ]


def greet(peers):
    barrier = pltpu.get_barrier_semaphore()
    for peer in peers:
        pl.semaphore_signal(barrier, inc=1, device_id=peer, device_id_type=pl.DeviceIdType.MESH)


def remote(src, dst, send, recv, peer):
    return pltpu.make_async_remote_copy(
        src_ref=src, dst_ref=dst, send_sem=send, recv_sem=recv, device_id=peer, device_id_type=pl.DeviceIdType.MESH
    )


class RingSum:
    def __init__(self, src, via_up, via_down, from_down, from_up, send, recv, me, above, below):
        self.src, self.me = src, me
        rows = src.shape[1]
        self.half = (pl.ds(0, rows // 2), pl.ds(rows // 2, rows // 2))
        self.via_up, self.via_down, self.from_down, self.from_up = via_up, via_down, from_down, from_up
        first, second = self.half
        far, near_up, near_down = up(me, 2), up(me), down(me)
        self.copies = [
            remote(src.at[far, first], via_up, send.at[0], recv.at[0], above),
            remote(src.at[far, second], via_down, send.at[1], recv.at[1], below),
            remote(src.at[near_up, second], from_down.at[second], send.at[2], recv.at[2], above),
            remote(src.at[near_down, first], from_up.at[first], send.at[3], recv.at[3], below),
            remote(src.at[near_up, first], from_down.at[first], send.at[4], recv.at[4], above),
            remote(src.at[near_down, second], from_up.at[second], send.at[5], recv.at[5], below),
        ]

    def far(self):
        for copy in self.copies[:2]:
            copy.start()

    def near(self):
        for copy in self.copies[2:4]:
            copy.start()

    def relay(self):
        first, second = self.half
        self.copies[0].wait_recv()
        near = up(self.me)
        self.src[near, first] = self.src[near, first] + self.via_up[...]
        self.copies[4].start()
        self.copies[1].wait_recv()
        near = down(self.me)
        self.src[near, second] = self.src[near, second] + self.via_down[...]
        self.copies[5].start()

    def arrive(self):
        for k in (2, 3, 4, 5):
            self.copies[k].wait_recv()

    def total(self, rows):
        return self.src[self.me, rows] + self.from_down[rows] + self.from_up[rows]

    def drain(self):
        for copy in self.copies:
            copy.wait_send()


class PlaneGather:
    def __init__(self, buf, send, recv, outer, inner, outer_up, outer_down, inner_up, inner_down):
        rows = buf.shape[2]
        first, second = pl.ds(0, rows // 2), pl.ds(rows // 2, rows // 2)
        row, below, above = buf.at[outer], buf.at[down(outer)], buf.at[up(outer)]

        def same(ref, k, peer):
            return remote(ref, ref, send.at[k], recv.at[k], peer)

        self.inner = [
            same(row.at[inner], 0, inner_up),
            same(row.at[inner], 1, inner_down),
            same(row.at[down(inner), first], 2, inner_up),
            same(row.at[up(inner), second], 3, inner_down),
        ]
        pieces = [inner, down(inner), up(inner), up(inner, 2)]
        self.direct = [(same(row.at[p], 4 + 2 * k, outer_up), same(row.at[p], 5 + 2 * k, outer_down)) for k, p in enumerate(pieces)]
        self.relays = [
            (same(below.at[p, first], 12 + 2 * k, outer_up), same(above.at[p, second], 13 + 2 * k, outer_down))
            for k, p in enumerate(pieces)
        ]

    def begin(self):
        for copy in self.inner[:2] + list(self.direct[0]):
            copy.start()

    def pass_inner(self):
        for k in range(2):
            self.inner[k].wait_recv()
            self.inner[2 + k].start()
            for copy in self.direct[1 + k]:
                copy.start()

    def last_inner(self):
        for k in (2, 3):
            self.inner[k].wait_recv()
        for copy in self.direct[3]:
            copy.start()

    def relay(self, piece):
        for k in range(2):
            self.direct[piece][k].wait_recv()
            self.relays[piece][k].start()

    def last(self):
        for pair in self.relays:
            for copy in pair:
                copy.wait_recv()

    def drain(self):
        for copy in self.inner + [copy for pair in self.direct + self.relays for copy in pair]:
            copy.wait_send()


def kernel(
    image, sens, bins, live, weights, fwd_right, fwd_left, back_left, back_right, natural, packed, phases, phases_t, out,
    image_buf, sens_buf, weight_buf, field, table, table_t, bins_row, bins_col, sums_a, sums_b, mids,
    via_up1, via_down1, from_down1, from_up1, via_up2, via_down2, from_down2, from_up2,
    mixed, gridded, all_a, all_b, planes_back, via_up, via_down, from_down, from_up, result,
    load_sem, weight_sem, table_sem, out_sem, bin_send, bin_recv, pair_send, pair_recv, ring_send, ring_recv,
    all_send, all_recv, slab_send, slab_recv, coil_send, coil_recv,
):
    core, chip, x, y = place()
    coil = lax.axis_index("coil")
    sibling = device(x, y, 1 - core)
    east, west = device(up(x), y, core), device(down(x), y, core)
    north, south = device(x, up(y), core), device(x, down(y), core)
    over, under = {"coil": up(coil)}, {"coil": down(coil)}
    others = [{"slab": lax.rem(chip + k, CHIPS) * 2 + core} for k in range(1, CHIPS)]
    peers = [sibling, over, under] + others
    greet(peers)

    def loads(i):
        return halved(image, image_buf, load_sem, i, 0) + halved(sens.at[0], sens_buf, load_sem, i, 2)

    def start_load(i, carry):
        for copy in loads(i):
            copy.start()
        return carry

    lax.fori_loop(0, PLANES, start_load, 0)
    fetch = pltpu.make_async_copy(phases.at[chip], table, table_sem.at[0])
    fetch_t = pltpu.make_async_copy(phases_t.at[chip], table_t, table_sem.at[1])
    fetch_weights = pltpu.make_async_copy(weights, weight_buf, weight_sem)
    fetch.start()
    bins_row[chip] = jnp.broadcast_to(bins[...].astype(F32), (8, SLOTS))
    spread = [remote(bins_row.at[chip], bins_row.at[chip], bin_send.at[k], bin_recv.at[k], others[k]) for k in range(CHIPS - 1)]

    def pair(i):
        return remote(field.at[2, i], field.at[core, i], pair_send.at[i], pair_recv.at[i], sibling)

    def plane_forward(i):
        for copy in loads(i):
            copy.wait()
        summed, differed = [], []
        for odd in range(2):
            rows = pl.ds(odd, TILE, stride=2)
            parts = []
            for half in range(2):
                image_re, image_im = image_buf[0, i, half, rows, :], image_buf[1, i, half, rows, :]
                sens_re, sens_im = sens_buf[0, i, half, rows, :], sens_buf[1, i, half, rows, :]
                parts.append((sens_re * image_re - sens_im * image_im, sens_re * image_im + sens_im * image_re))
            summed.append(jnp.concatenate([parts[0][k] + parts[1][k] for k in range(2)], 1))
            differed.append(jnp.concatenate([parts[0][k] - parts[1][k] for k in range(2)], 1))
        even_z = dot(wide(jnp.concatenate(summed, 0)), fwd_right[0])
        odd_z = dot(wide(jnp.concatenate(differed, 0)), fwd_right[1])
        parts = []
        for odd in range(2):
            rows = slice(odd * TILE, (odd + 1) * TILE)
            stacked = jnp.concatenate(
                [
                    jnp.concatenate([even_z[rows, :TILE], odd_z[rows, :TILE]], 1),
                    jnp.concatenate([even_z[rows, TILE:], odd_z[rows, TILE:]], 1),
                ],
                0,
            )
            parts.append(dot(fwd_left[odd], tall(stacked)))
        for side, values in enumerate((parts[0] + parts[1], parts[0] - parts[1])):
            values = values.reshape(2, 8, 2, 8, N)
            for part in range(2):
                field[2 * core, i, pl.ds(8 * side, 8), part] = values[part, :, 0]
                field[2 - core, i, pl.ds(8 * side, 8), part] = values[part, :, 1]

    def plane_and_pair(i, carry):
        plane_forward(i)
        pair(i).start()
        return carry

    plane_forward(0)
    pl.semaphore_wait(pltpu.get_barrier_semaphore(), len(peers))
    pair(0).start()
    for copy in spread:
        copy.start()
    lax.fori_loop(1, PLANES, plane_and_pair, 0)
    fetch_weights.start()
    fetch_t.start()
    fetch.wait()
    for copy in spread:
        copy.wait_recv()
    bins_col[...] = bins_row[...].reshape(CHIPS * 8, SLOTS).T
    lane = lax.broadcasted_iota(jnp.int32, (SLOTS, TILE), 1)

    def column(p):
        return jnp.sum(jnp.where(lane == 8 * p, bins_col[...], 0.0), axis=1, keepdims=True).astype(jnp.int32)

    own_side = jnp.broadcast_to(column(chip) % 2, (SLOTS, TILE)) == 1

    def slab_sums(px, py):
        p = py * RING + px
        index = column(p)
        kx, ky, side = index // 16, (index // 2) % 8, index % 2
        hot = jnp.where(lax.broadcasted_iota(jnp.int32, (SLOTS, N), 1) == kx, 1.0, 0.0).astype(BF16)
        phase = dot(hot, table[...])
        row = lax.broadcasted_iota(jnp.int32, (SLOTS, 4 * TILE), 1) % 8
        phase = jnp.where(row == ky, phase, 0.0).astype(BF16)
        mats = []
        for k in range(2):
            cosine, sine = phase[:, 2 * k * TILE : (2 * k + 1) * TILE], phase[:, (2 * k + 1) * TILE : (2 * k + 2) * TILE]
            mats.append(jnp.concatenate([jnp.concatenate([cosine, sine], 1), jnp.concatenate([-sine, cosine], 1)], 0))
        rows = jnp.concatenate([field[c, :, p, part].reshape(64, N) for part in range(2) for c in range(2)], 0)
        sums = dot(jnp.concatenate([mats[0], mats[1], mats[0]], 1), tall(rows))
        low_lane = jnp.where(lane < 64, 0, 1) == side
        sums_re = jnp.where(low_lane, sums[:SLOTS, :TILE], sums[:SLOTS, TILE:])
        sums_im = jnp.where(low_lane, sums[SLOTS:, :TILE], sums[SLOTS:, TILE:])
        for g in range(GROUPS):
            sums_a[g, px, pl.ds(py * SPAN, SPAN)] = sums_re[g * SPAN : (g + 1) * SPAN]
            sums_b[g, py, pl.ds(px * SPAN, SPAN)] = sums_im[g * SPAN : (g + 1) * SPAN]

    def over_slabs(one):
        def far_column(k, carry):
            one(up(x, 2), up(y, k))
            return carry

        def far_row(k, carry):
            one(up(x, 3 + k), up(y, 2))
            return carry

        def near(k, carry):
            one(up(x, 3 + k % 3), up(y, 3 + k // 3))
            return carry

        def far():
            lax.fori_loop(0, 4, far_column, 0, unroll=2)
            lax.fori_loop(0, 3, far_row, 0, unroll=3)

        return far, lambda start, stop, unroll: lax.fori_loop(start, stop, near, 0, unroll=unroll)

    first, second = [], []
    for g in range(GROUPS):
        for half in range(2):
            k = 2 * g + half
            ring = (x, east, west) if half == 0 else (y, north, south)
            src = (sums_a, sums_b)[half].at[g]
            first.append(RingSum(src, via_up1.at[k], via_down1.at[k], from_down1.at[k], from_up1.at[k], ring_send.at[k], ring_recv.at[k], *ring))
            ring = (y, north, south) if half == 0 else (x, east, west)
            j = 2 * GROUPS + k
            second.append(RingSum(mids.at[k], via_up2.at[k], via_down2.at[k], from_down2.at[k], from_up2.at[k], ring_send.at[j], ring_recv.at[j], *ring))
    gathers = []
    for g in range(GROUPS):
        gathers.append(
            (
                PlaneGather(all_a.at[g], all_send.at[2 * g], all_recv.at[2 * g], x, y, east, west, north, south),
                PlaneGather(all_b.at[g], all_send.at[2 * g + 1], all_recv.at[2 * g + 1], y, x, north, south, east, west),
            )
        )

    def rings(which, g, action):
        for ring in which[2 * g : 2 * g + 2]:
            getattr(ring, action)()

    def middle(g):
        for k in (2 * g, 2 * g + 1):
            first[k].arrive()
            for m in range(RING):
                mids[k, m] = first[k].total(pl.ds(m * SPAN, SPAN))
            second[k].far()
            second[k].near()

    def grid(g):
        rings(second, g, "arrive")
        values = jnp.concatenate([second[2 * g].total(pl.ds(0, SPAN)), second[2 * g + 1].total(pl.ds(0, SPAN))], 0)
        upper = own_side[g * SPAN : (g + 1) * SPAN]
        upper = jnp.concatenate([upper] * 4, 0)
        high = values.astype(BF16).astype(F32)
        both = jnp.concatenate([high, values - high], 0)
        both = jnp.concatenate([jnp.where(upper, 0.0, both), jnp.where(upper, both, 0.0)], 1).astype(BF16)
        mixed[...] = dot(both, natural[...]).reshape(4, SPAN, TILE)

        def unit(k, carry):
            row = lax.broadcasted_iota(jnp.int32, (32, TILE), 0) % 8
            rows = [pl.ds(16 * k + 8 * u, 8) for u in range(2)]
            low = [mixed[:, r].reshape(32, TILE).astype(BF16) for r in rows]
            none = jnp.zeros((32, TILE), BF16)
            lhs = jnp.concatenate([jnp.concatenate([low[0], none], 1), jnp.concatenate([none, low[1]], 1)], 0)
            mat = jnp.concatenate([weight_buf[pl.ds(g * SPAN + 16 * k + 8 * u, 8)].reshape(8 * TILE, TILE) for u in range(2)], 1)
            spread = lax.dot_general(lhs, mat, (((1,), (1,)), ((), ())), preferred_element_type=F32)
            masked = []
            for u in range(2):
                samples = jnp.zeros((32, TILE), F32)
                for j in range(8):
                    samples = jnp.where(row == j, spread[32 * u : 32 * u + 32, j * TILE : (j + 1) * TILE], samples)
                samples = samples[:16] + samples[16:]
                high = samples.astype(BF16).astype(F32)
                both = jnp.concatenate([high, samples - high], 0)
                masked.append(jnp.concatenate([jnp.where(row == j, both, 0.0).astype(BF16) for j in range(8)], 1))
            back = dot(jnp.concatenate(masked, 0), mat)
            for u in range(2):
                values = back[32 * u : 32 * u + 32, u * TILE : (u + 1) * TILE]
                values = values[:16] + values[16:]
                gridded[0, rows[u]] = values[:8]
                gridded[1, rows[u]] = values[8:]
            return carry

        lax.fori_loop(0, SPAN // 16, unit, 0, unroll=4)
        high, low = split(gridded[...].reshape(2 * SPAN, TILE))
        back = dot(jnp.concatenate([high, low], 0), packed[...])
        back = jnp.where(upper, back[:, TILE:], back[:, :TILE])
        back = back[: 2 * SPAN] + back[2 * SPAN :]
        slot = g * SPAN + lax.broadcasted_iota(jnp.int32, (2 * SPAN, TILE), 0) % SPAN
        back = jnp.where(slot < live[0], back, 0.0)
        all_a[g, x, y] = back[:SPAN]
        all_b[g, y, x] = back[SPAN:]

    def slab_pair(p):
        return remote(planes_back.at[2, p], planes_back.at[core, p], slab_send.at[p], slab_recv.at[p], sibling)

    def slab_back(g, px, py):
        p = py * RING + px
        side = column(p)[g * SPAN : (g + 1) * SPAN] % 2
        index = bins_row[p, 0:1, pl.ds(g * SPAN, SPAN)].astype(jnp.int32)
        kx, ky = index // 16, (index // 2) % 8
        hot = jnp.where(lax.broadcasted_iota(jnp.int32, (N, SPAN), 0) == kx, 1.0, 0.0).astype(BF16)
        phase = dot(table_t[...], hot)
        row = lax.broadcasted_iota(jnp.int32, (4 * TILE, SPAN), 0) % 8
        phase = jnp.where(row == ky, phase, 0.0).astype(BF16)
        mats = []
        for k in range(2):
            cosine, sine = phase[2 * k * TILE : (2 * k + 1) * TILE], phase[(2 * k + 1) * TILE : (2 * k + 2) * TILE]
            mats.append(jnp.concatenate([jnp.concatenate([cosine, -sine], 1), jnp.concatenate([sine, cosine], 1)], 0))
        tiles = jnp.concatenate([all_a[g, px, py], all_b[g, py, px]], 0)
        low_lane = jnp.where(lane[:SPAN] < 64, 0, 1) == side
        low_lane = jnp.concatenate([low_lane, low_lane], 0)
        tiles = jnp.concatenate([jnp.where(low_lane, tiles, 0.0), jnp.where(low_lane, 0.0, tiles)], 1)
        sums = dot(jnp.concatenate([mats[0], mats[1], mats[0]], 1), tall(tiles))
        sums = sums.reshape(2, 2, PLANES, 8, N)
        for part in range(2):
            for source, slot in ((0, 2 * core), (1, 2 - core)):
                values = sums[part, source]
                if g > 0:
                    values = values + planes_back[slot, p, :, part]
                planes_back[slot, p, :, part] = values
        if g == GROUPS - 1:
            slab_pair(p).start()

    far_sums, near_sums = over_slabs(slab_sums)

    def arrived(i, carry):
        pair(i).wait_recv()
        return carry

    lax.fori_loop(0, PLANES, arrived, 0)
    far_sums()
    rings(first, 0, "far")
    near_sums(0, 4, 2)
    near_sums(5, 9, 2)
    rings(first, 0, "near")
    slab_sums(x, y)
    rings(first, 0, "relay")
    if GROUPS == 2:
        rings(first, 1, "far")
    middle(0)
    if GROUPS == 2:
        rings(first, 1, "near")
        rings(first, 1, "relay")
    rings(second, 0, "relay")
    fetch_weights.wait()
    fetch_t.wait()
    grid(0)

    def both(g, action, *args):
        for gather in gathers[g]:
            getattr(gather, action)(*args)

    both(0, "begin")
    if GROUPS == 2:
        middle(1)
        both(0, "pass_inner")
        rings(second, 1, "relay")
        both(0, "relay", 0)
        grid(1)
        both(1, "begin")
    else:
        both(0, "pass_inner")
        both(0, "relay", 0)
    both(0, "last_inner")
    both(0, "relay", 1)
    both(0, "relay", 2)
    if GROUPS == 2:
        both(1, "pass_inner")
    both(0, "relay", 3)
    for g in range(GROUPS):
        far_back, near_back = over_slabs(functools.partial(slab_back, g))
        if g == 1:
            both(1, "last_inner")
            both(1, "relay", 1)
            both(1, "relay", 2)
            both(1, "relay", 3)
        near_back(0, 9, 3)
        if g == 0 and GROUPS == 2:
            both(1, "relay", 0)
        both(g, "last")
        far_back()

    def slabs_arrived(p, carry):
        slab_pair(p).wait_recv()
        return carry

    lax.fori_loop(0, CHIPS, slabs_arrived, 0)

    term = image_buf
    quarter = N // RING
    far, near_up, near_down = up(coil, 2), up(coil), down(coil)

    def share(part, i, q):
        return term.at[part, i, :, pl.ds(pl.multiple_of(q * quarter, quarter), quarter)]

    def coil_copy(i, k):
        source, target, peer = (
            (share(0, i, far), via_up.at[i], over),
            (share(1, i, far), via_down.at[i], under),
            (share(1, i, near_up), from_down.at[i, 1], over),
            (share(0, i, near_down), from_up.at[i, 0], under),
            (share(0, i, near_up), from_down.at[i, 0], over),
            (share(1, i, near_down), from_up.at[i, 1], under),
        )[k]
        return remote(source, target, coil_send.at[i, k], coil_recv.at[i, k], peer)

    def coil_relay(i):
        coil_copy(i, 0).wait_recv()
        ref = share(0, i, near_up)
        ref[...] = ref[...] + via_up[i]
        coil_copy(i, 4).start()
        coil_copy(i, 1).wait_recv()
        ref = share(1, i, near_down)
        ref[...] = ref[...] + via_down[i]
        coil_copy(i, 5).start()

    def plane_back(i, carry):
        near_half, far_half = planes_back[pl.ds(0, 2), pl.ds(0, 8), i], planes_back[pl.ds(0, 2), pl.ds(8, 8), i]
        even = dot(back_left[0], tall((near_half + far_half).reshape(N, N)))
        odd = dot(back_left[1], tall((near_half - far_half).reshape(N, N)))
        halves_z = []
        for k in range(2):
            lanes = slice(k * TILE, (k + 1) * TILE)
            stacked = jnp.concatenate([jnp.concatenate([v[:TILE, lanes], v[TILE:, lanes]], 1) for v in (even, odd)], 0)
            halves_z.append(dot(wide(stacked), back_right[k]))
        for half, values in enumerate((halves_z[0] + halves_z[1], halves_z[0] - halves_z[1])):
            for odd in range(2):
                rows = slice(odd * TILE, (odd + 1) * TILE)
                field_re, field_im = values[rows, :TILE], values[rows, TILE:]
                every = pl.ds(odd, TILE, stride=2)
                sens_re, sens_im = sens_buf[0, i, half, every, :], sens_buf[1, i, half, every, :]
                term[0, i, half, every, :] = sens_re * field_re + sens_im * field_im
                term[1, i, half, every, :] = sens_re * field_im - sens_im * field_re
        for k in range(4):
            coil_copy(i, k).start()

        @pl.when(i > 0)
        def _():
            coil_relay(i - 1)

        return carry

    lax.fori_loop(0, PLANES, plane_back, 0)
    coil_relay(PLANES - 1)

    def store(i):
        return pltpu.make_async_copy(result.at[:, i], out.at[:, i], out_sem.at[i])

    def collect(i, carry):
        for k in (2, 3, 4, 5):
            coil_copy(i, k).wait_recv()
        for part in range(2):
            total = share(part, i, coil)[...] + from_down[i, part] + from_up[i, part]
            for half in range(2):
                result[part, i, :, half * TILE : (half + 1) * TILE] = total[half]
        store(i).start()
        for k in range(6):
            coil_copy(i, k).wait_send()
        return carry

    def finished(i, carry):
        store(i).wait()
        pair(i).wait_send()
        return carry

    def slabs_sent(p, carry):
        slab_pair(p).wait_send()
        return carry

    lax.fori_loop(0, PLANES, collect, 0)
    lax.fori_loop(0, PLANES, finished, 0)
    lax.fori_loop(0, CHIPS, slabs_sent, 0)
    for ring in first + second:
        ring.drain()
    for g in range(GROUPS):
        both(g, "drain")
    for copy in spread:
        copy.wait_send()


def fused(image, sens, bins, live, weights, tab):
    quarter = N // RING
    rings = 2 * GROUPS
    vmem = pl.BlockSpec(memory_space=pltpu.VMEM)
    hbm = pl.BlockSpec(memory_space=pl.ANY)
    smem = pl.BlockSpec(memory_space=pltpu.SMEM)
    return pl.pallas_call(
        kernel,
        out_shape=jax.ShapeDtypeStruct((2, PLANES, quarter, N), F32),
        in_specs=[hbm, hbm, vmem, smem, hbm] + [vmem] * 6 + [hbm] * 2,
        out_specs=hbm,
        scratch_shapes=[
            pltpu.VMEM((2, PLANES, 2, N, TILE), F32),
            pltpu.VMEM((2, PLANES, 2, N, TILE), F32),
            pltpu.VMEM((SLOTS, TILE, TILE), BF16),
            pltpu.VMEM((3, PLANES, CHIPS, 2, 8, N), F32),
            pltpu.VMEM((N, 4 * TILE), BF16),
            pltpu.VMEM((4 * TILE, N), BF16),
            pltpu.VMEM((CHIPS, 8, SLOTS), F32),
            pltpu.VMEM((SLOTS, CHIPS * 8), F32),
            pltpu.VMEM((GROUPS, RING, RING * SPAN, TILE), F32),
            pltpu.VMEM((GROUPS, RING, RING * SPAN, TILE), F32),
            pltpu.VMEM((rings, RING, SPAN, TILE), F32),
            pltpu.VMEM((rings, 2 * SPAN, TILE), F32),
            pltpu.VMEM((rings, 2 * SPAN, TILE), F32),
            pltpu.VMEM((rings, 4 * SPAN, TILE), F32),
            pltpu.VMEM((rings, 4 * SPAN, TILE), F32),
            pltpu.VMEM((rings, SPAN // 2, TILE), F32),
            pltpu.VMEM((rings, SPAN // 2, TILE), F32),
            pltpu.VMEM((rings, SPAN, TILE), F32),
            pltpu.VMEM((rings, SPAN, TILE), F32),
            pltpu.VMEM((4, SPAN, TILE), F32),
            pltpu.VMEM((2, SPAN, TILE), F32),
            pltpu.VMEM((GROUPS, RING, RING, SPAN, TILE), F32),
            pltpu.VMEM((GROUPS, RING, RING, SPAN, TILE), F32),
            pltpu.VMEM((3, CHIPS, PLANES, 2, 8, N), F32),
            pltpu.VMEM((PLANES, 2, quarter, TILE), F32),
            pltpu.VMEM((PLANES, 2, quarter, TILE), F32),
            pltpu.VMEM((PLANES, 2, 2, quarter, TILE), F32),
            pltpu.VMEM((PLANES, 2, 2, quarter, TILE), F32),
            pltpu.VMEM((2, PLANES, quarter, N), F32),
            pltpu.SemaphoreType.DMA((PLANES, 4)),
            pltpu.SemaphoreType.DMA,
            pltpu.SemaphoreType.DMA((2,)),
            pltpu.SemaphoreType.DMA((PLANES,)),
            pltpu.SemaphoreType.DMA((CHIPS - 1,)),
            pltpu.SemaphoreType.DMA((CHIPS - 1,)),
            pltpu.SemaphoreType.DMA((PLANES,)),
            pltpu.SemaphoreType.DMA((PLANES,)),
            pltpu.SemaphoreType.DMA((2 * rings, 6)),
            pltpu.SemaphoreType.DMA((2 * rings, 6)),
            pltpu.SemaphoreType.DMA((rings, 20)),
            pltpu.SemaphoreType.DMA((rings, 20)),
            pltpu.SemaphoreType.DMA((CHIPS,)),
            pltpu.SemaphoreType.DMA((CHIPS,)),
            pltpu.SemaphoreType.DMA((PLANES, 6)),
            pltpu.SemaphoreType.DMA((PLANES, 6)),
        ],
        compiler_params=pltpu.CompilerParams(collective_id=0, has_side_effects=True, vmem_limit_bytes=VMEM_LIMIT),
    )(
        image, sens, bins, live, weights, tab["fwd_right"], tab["fwd_left"], tab["back_left"], tab["back_right"],
        tab["natural"], tab["packed"], tab["phases"], tab["phases_t"],
    )


def body(image, sens, weights, bins, counts):
    tab = {name: jnp.asarray(table) for name, table in tables().items()}
    return fused(image, sens, bins.reshape(1, SLOTS), counts, weights, tab)


def solution(mesh):
    in_specs = (
        P(None, "slab", None, None),
        P("coil", None, "slab", None, None),
        P("slab", None, None),
        P("slab"),
        P("slab"),
    )
    out_specs = P(None, "slab", "coil", None)
    return jax.shard_map(body, mesh=mesh, in_specs=in_specs, out_specs=out_specs, check_vma=False)
```

profile of v0, /device:TPU:1, one launch (start us, length us, event | category | flops | bytes accessed | tf_op | source)
XLA Modules:
  0.0 134.7 jit_solution(5032131179613806818)
XLA Ops:
  0.7 131.8 %shard_map.127 = f32[2,8,64,256]{3,2,1,0:T(8,128)} custom-call(f32[2,8,256,256]{3,2,1,0:T(8,128)} %image.1, f32[1,2,8,256,256]{4,3,2,1,0:T(8,128)} %sens.1, s32[1,256]{1,0:T(1,128)} %bitcast.1, s32[1]{0:T(128)S(6)} %copy.15.live, bf16[256,128,128]{2,1,0:T(8,128)(2,1)} %weights.1, bf16[2,768,256]{2,1,0:T(8,128)(2,1)} %constant.16.clone.fwd_right, ...), custom_call_target="tpu_custom_call" | custom-call | tf_op jit(solution)/shard_map/pallas_call | solution.py:645
  132.4 2.3 %copy.16 = f32[2,8,64,256]{3,2,1,0:T(8,128)} copy(f32[2,8,64,256]{3,2,1,0:T(8,128)} %shard_map.127) | data formatting | bytes 2097152
where the time goes:
time: 135 us
  Pallas kernels  132 us (98%)
  local copies, waits for them, and re-layouts  2.29 us (2%)
    pallas_call x1, Pallas kernels, fused(): pl.pallas_call(kernel, out_shape=jax.ShapeDtypeStruct((2, PLANES, quarter...  132 us

commit v1 on v0

--- a/solution.py
+++ b/solution.py
@@ -185,6 +185,30 @@
             copy.wait_send()
 
 
+class RingDirect:
+    def __init__(self, src, slots, send, recv, me, peers):
+        self.src, self.slots, self.me = src, slots, me
+        self.copies = [
+            remote(src.at[up(me, step)], slots.at[k], send.at[k], recv.at[k], peer)
+            for k, (step, peer) in enumerate(zip((2, 1, 3), peers))
+        ]
+
+    def begin(self):
+        for copy in self.copies:
+            copy.start()
+
+    def arrive(self):
+        for copy in self.copies:
+            copy.wait_recv()
+
+    def total(self):
+        return self.src[self.me] + self.slots[0] + self.slots[1] + self.slots[2]
+
+    def drain(self):
+        for copy in self.copies:
+            copy.wait_send()
+
+
 class PlaneGather:
     def __init__(self, buf, send, recv, outer, inner, outer_up, outer_down, inner_up, inner_down):
         rows = buf.shape[2]
@@ -229,10 +253,9 @@
             self.direct[piece][k].wait_recv()
             self.relays[piece][k].start()
 
-    def last(self):
-        for pair in self.relays:
-            for copy in pair:
-                copy.wait_recv()
+    def last(self, piece):
+        for copy in self.relays[piece]:
+            copy.wait_recv()
 
     def drain(self):
         for copy in self.inner + [copy for pair in self.direct + self.relays for copy in pair]:
@@ -240,11 +263,11 @@
 
 
 def kernel(
-    image, sens, bins, live, weights, fwd_right, fwd_left, back_left, back_right, natural, packed, phases, phases_t, out,
-    image_buf, sens_buf, weight_buf, field, table, table_t, bins_row, bins_col, sums_a, sums_b, mids,
-    via_up1, via_down1, from_down1, from_up1, via_up2, via_down2, from_down2, from_up2,
-    mixed, gridded, all_a, all_b, planes_back, via_up, via_down, from_down, from_up, result,
-    load_sem, weight_sem, table_sem, out_sem, bin_send, bin_recv, pair_send, pair_recv, ring_send, ring_recv,
+    image, sens, bins, live, weights, fwd_right_hbm, fwd_left_hbm, back_left_hbm, back_right_hbm, natural_hbm, packed_hbm, phases, phases_t, out,
+    fwd_right, fwd_left, back_left, back_right, natural, packed, image_buf, sens_buf, weight_buf, field, table, table_t, bins_row, bins_col, sums_a, sums_b, mids,
+    via_up1, via_down1, from_down1, from_up1, slots2,
+    mixed, gridded, back_phase, all_a, all_b, planes_back, via_up, via_down, from_down, from_up, result,
+    load_sem, weight_sem, table_sem, out_sem, bin_send, bin_recv, pair_send, pair_recv, ring_send, ring_recv, share_send, share_recv,
     all_send, all_recv, slab_send, slab_recv, coil_send, coil_recv,
 ):
     core, chip, x, y = place()
@@ -255,8 +278,6 @@
     over, under = {"coil": up(coil)}, {"coil": down(coil)}
     others = [{"slab": lax.rem(chip + k, CHIPS) * 2 + core} for k in range(1, CHIPS)]
     peers = [sibling, over, under] + others
-    greet(peers)
-
     def loads(i):
         return halved(image, image_buf, load_sem, i, 0) + halved(sens.at[0], sens_buf, load_sem, i, 2)
 
@@ -265,10 +286,21 @@
             copy.start()
         return carry
 
-    lax.fori_loop(0, PLANES, start_load, 0)
+    early = [pltpu.make_async_copy(fwd_right_hbm, fwd_right, table_sem.at[2]), pltpu.make_async_copy(fwd_left_hbm, fwd_left, table_sem.at[3])]
+    late = [
+        pltpu.make_async_copy(source, target, table_sem.at[4 + k])
+        for k, (source, target) in enumerate(
+            ((back_left_hbm, back_left), (back_right_hbm, back_right), (natural_hbm, natural), (packed_hbm, packed))
+        )
+    ]
     fetch = pltpu.make_async_copy(phases.at[chip], table, table_sem.at[0])
     fetch_t = pltpu.make_async_copy(phases_t.at[chip], table_t, table_sem.at[1])
     fetch_weights = pltpu.make_async_copy(weights, weight_buf, weight_sem)
+    start_load(0, 0)
+    for copy in early:
+        copy.start()
+    greet(peers)
+    lax.fori_loop(1, PLANES, start_load, 0)
     fetch.start()
     bins_row[chip] = jnp.broadcast_to(bins[...].astype(F32), (8, SLOTS))
     spread = [remote(bins_row.at[chip], bins_row.at[chip], bin_send.at[k], bin_recv.at[k], others[k]) for k in range(CHIPS - 1)]
@@ -313,32 +345,35 @@
         pair(i).start()
         return carry
 
+    for copy in early:
+        copy.wait()
     plane_forward(0)
     pl.semaphore_wait(pltpu.get_barrier_semaphore(), len(peers))
     pair(0).start()
     for copy in spread:
         copy.start()
     lax.fori_loop(1, PLANES, plane_and_pair, 0)
+    fetch_t.start()
     fetch_weights.start()
-    fetch_t.start()
+    for copy in late:
+        copy.start()
     fetch.wait()
     for copy in spread:
         copy.wait_recv()
     bins_col[...] = bins_row[...].reshape(CHIPS * 8, SLOTS).T
-    lane = lax.broadcasted_iota(jnp.int32, (SLOTS, TILE), 1)
-
-    def column(p):
-        return jnp.sum(jnp.where(lane == 8 * p, bins_col[...], 0.0), axis=1, keepdims=True).astype(jnp.int32)
-
-    own_side = jnp.broadcast_to(column(chip) % 2, (SLOTS, TILE)) == 1
-
-    def slab_sums(px, py):
+    lane = lax.broadcasted_iota(jnp.int32, (SPAN, TILE), 1)
+
+    def column(p, g):
+        values = bins_col[pl.ds(g * SPAN, SPAN)]
+        return jnp.sum(jnp.where(lane == 8 * p, values, 0.0), axis=1, keepdims=True).astype(jnp.int32)
+
+    def slab_sums(g, px, py):
         p = py * RING + px
-        index = column(p)
+        index = column(p, g)
         kx, ky, side = index // 16, (index // 2) % 8, index % 2
-        hot = jnp.where(lax.broadcasted_iota(jnp.int32, (SLOTS, N), 1) == kx, 1.0, 0.0).astype(BF16)
+        hot = jnp.where(lax.broadcasted_iota(jnp.int32, (SPAN, N), 1) == kx, 1.0, 0.0).astype(BF16)
         phase = dot(hot, table[...])
-        row = lax.broadcasted_iota(jnp.int32, (SLOTS, 4 * TILE), 1) % 8
+        row = lax.broadcasted_iota(jnp.int32, (SPAN, 4 * TILE), 1) % 8
         phase = jnp.where(row == ky, phase, 0.0).astype(BF16)
         mats = []
         for k in range(2):
@@ -347,11 +382,8 @@
         rows = jnp.concatenate([field[c, :, p, part].reshape(64, N) for part in range(2) for c in range(2)], 0)
         sums = dot(jnp.concatenate([mats[0], mats[1], mats[0]], 1), tall(rows))
         low_lane = jnp.where(lane < 64, 0, 1) == side
-        sums_re = jnp.where(low_lane, sums[:SLOTS, :TILE], sums[:SLOTS, TILE:])
-        sums_im = jnp.where(low_lane, sums[SLOTS:, :TILE], sums[SLOTS:, TILE:])
-        for g in range(GROUPS):
-            sums_a[g, px, pl.ds(py * SPAN, SPAN)] = sums_re[g * SPAN : (g + 1) * SPAN]
-            sums_b[g, py, pl.ds(px * SPAN, SPAN)] = sums_im[g * SPAN : (g + 1) * SPAN]
+        sums_a[g, px, pl.ds(py * SPAN, SPAN)] = jnp.where(low_lane, sums[:SPAN, :TILE], sums[:SPAN, TILE:])
+        sums_b[g, py, pl.ds(px * SPAN, SPAN)] = jnp.where(low_lane, sums[SPAN:, :TILE], sums[SPAN:, TILE:])
 
     def over_slabs(one):
         def far_column(k, carry):
@@ -366,11 +398,11 @@
             one(up(x, 3 + k % 3), up(y, 3 + k // 3))
             return carry
 
-        def far():
-            lax.fori_loop(0, 4, far_column, 0, unroll=2)
-            lax.fori_loop(0, 3, far_row, 0, unroll=3)
-
-        return far, lambda start, stop, unroll: lax.fori_loop(start, stop, near, 0, unroll=unroll)
+        return (
+            lambda unroll: lax.fori_loop(0, 4, far_column, 0, unroll=unroll),
+            lambda unroll: lax.fori_loop(0, 3, far_row, 0, unroll=unroll),
+            lambda start, stop, unroll: lax.fori_loop(start, stop, near, 0, unroll=unroll),
+        )
 
     first, second = [], []
     for g in range(GROUPS):
@@ -379,9 +411,8 @@
             ring = (x, east, west) if half == 0 else (y, north, south)
             src = (sums_a, sums_b)[half].at[g]
             first.append(RingSum(src, via_up1.at[k], via_down1.at[k], from_down1.at[k], from_up1.at[k], ring_send.at[k], ring_recv.at[k], *ring))
-            ring = (y, north, south) if half == 0 else (x, east, west)
-            j = 2 * GROUPS + k
-            second.append(RingSum(mids.at[k], via_up2.at[k], via_down2.at[k], from_down2.at[k], from_up2.at[k], ring_send.at[j], ring_recv.at[j], *ring))
+            me, others_k = (y, (device(x, up(y, 2), core), north, south)) if half == 0 else (x, (device(up(x, 2), y, core), east, west))
+            second.append(RingDirect(mids.at[k], slots2.at[k], share_send.at[k], share_recv.at[k], me, others_k))
     gathers = []
     for g in range(GROUPS):
         gathers.append(
@@ -400,19 +431,21 @@
             first[k].arrive()
             for m in range(RING):
                 mids[k, m] = first[k].total(pl.ds(m * SPAN, SPAN))
-            second[k].far()
-            second[k].near()
-
-    def grid(g):
+            second[k].begin()
+
+    def own_upper(g):
+        return jnp.concatenate([jnp.broadcast_to(column(chip, g) % 2, (SPAN, TILE)) == 1] * 4, 0)
+
+    def grid_begin(g):
         rings(second, g, "arrive")
-        values = jnp.concatenate([second[2 * g].total(pl.ds(0, SPAN)), second[2 * g + 1].total(pl.ds(0, SPAN))], 0)
-        upper = own_side[g * SPAN : (g + 1) * SPAN]
-        upper = jnp.concatenate([upper] * 4, 0)
+        values = jnp.concatenate([second[2 * g].total(), second[2 * g + 1].total()], 0)
+        upper = own_upper(g)
         high = values.astype(BF16).astype(F32)
         both = jnp.concatenate([high, values - high], 0)
         both = jnp.concatenate([jnp.where(upper, 0.0, both), jnp.where(upper, both, 0.0)], 1).astype(BF16)
         mixed[...] = dot(both, natural[...]).reshape(4, SPAN, TILE)
 
+    def grid_units(g, start, stop):
         def unit(k, carry):
             row = lax.broadcasted_iota(jnp.int32, (32, TILE), 0) % 8
             rows = [pl.ds(16 * k + 8 * u, 8) for u in range(2)]
@@ -438,7 +471,10 @@
                 gridded[1, rows[u]] = values[8:]
             return carry
 
-        lax.fori_loop(0, SPAN // 16, unit, 0, unroll=4)
+        lax.fori_loop(start, stop, unit, 0, unroll=4)
+
+    def grid_end(g):
+        upper = own_upper(g)
         high, low = split(gridded[...].reshape(2 * SPAN, TILE))
         back = dot(jnp.concatenate([high, low], 0), packed[...])
         back = jnp.where(upper, back[:, TILE:], back[:, :TILE])
@@ -451,21 +487,28 @@
     def slab_pair(p):
         return remote(planes_back.at[2, p], planes_back.at[core, p], slab_send.at[p], slab_recv.at[p], sibling)
 
+    def prepare(g):
+        def one(p, carry):
+            index = bins_row[p, 0:1, pl.ds(g * SPAN, SPAN)].astype(jnp.int32)
+            kx, ky = index // 16, (index // 2) % 8
+            hot = jnp.where(lax.broadcasted_iota(jnp.int32, (N, SPAN), 0) == kx, 1.0, 0.0).astype(BF16)
+            phase = dot(table_t[...], hot)
+            row = lax.broadcasted_iota(jnp.int32, (4 * TILE, SPAN), 0) % 8
+            back_phase[g, p] = jnp.where(row == ky, phase, 0.0).astype(BF16)
+            return carry
+
+        return lambda start, stop: lax.fori_loop(start, stop, one, 0, unroll=2)
+
     def slab_back(g, px, py):
         p = py * RING + px
-        side = column(p)[g * SPAN : (g + 1) * SPAN] % 2
-        index = bins_row[p, 0:1, pl.ds(g * SPAN, SPAN)].astype(jnp.int32)
-        kx, ky = index // 16, (index // 2) % 8
-        hot = jnp.where(lax.broadcasted_iota(jnp.int32, (N, SPAN), 0) == kx, 1.0, 0.0).astype(BF16)
-        phase = dot(table_t[...], hot)
-        row = lax.broadcasted_iota(jnp.int32, (4 * TILE, SPAN), 0) % 8
-        phase = jnp.where(row == ky, phase, 0.0).astype(BF16)
+        side = column(p, g) % 2
+        phase = back_phase[g, p]
         mats = []
         for k in range(2):
             cosine, sine = phase[2 * k * TILE : (2 * k + 1) * TILE], phase[(2 * k + 1) * TILE : (2 * k + 2) * TILE]
             mats.append(jnp.concatenate([jnp.concatenate([cosine, -sine], 1), jnp.concatenate([sine, cosine], 1)], 0))
         tiles = jnp.concatenate([all_a[g, px, py], all_b[g, py, px]], 0)
-        low_lane = jnp.where(lane[:SPAN] < 64, 0, 1) == side
+        low_lane = jnp.where(lane < 64, 0, 1) == side
         low_lane = jnp.concatenate([low_lane, low_lane], 0)
         tiles = jnp.concatenate([jnp.where(low_lane, tiles, 0.0), jnp.where(low_lane, 0.0, tiles)], 1)
         sums = dot(jnp.concatenate([mats[0], mats[1], mats[0]], 1), tall(tiles))
@@ -479,64 +522,81 @@
         if g == GROUPS - 1:
             slab_pair(p).start()
 
-    far_sums, near_sums = over_slabs(slab_sums)
-
     def arrived(i, carry):
         pair(i).wait_recv()
         return carry
-
-    lax.fori_loop(0, PLANES, arrived, 0)
-    far_sums()
-    rings(first, 0, "far")
-    near_sums(0, 4, 2)
-    near_sums(5, 9, 2)
-    rings(first, 0, "near")
-    slab_sums(x, y)
-    rings(first, 0, "relay")
-    if GROUPS == 2:
-        rings(first, 1, "far")
-    middle(0)
-    if GROUPS == 2:
-        rings(first, 1, "near")
-        rings(first, 1, "relay")
-    rings(second, 0, "relay")
-    fetch_weights.wait()
-    fetch_t.wait()
-    grid(0)
 
     def both(g, action, *args):
         for gather in gathers[g]:
             getattr(gather, action)(*args)
 
+    sums = [over_slabs(functools.partial(slab_sums, g)) for g in range(GROUPS)]
+    backs = [over_slabs(functools.partial(slab_back, g)) for g in range(GROUPS)]
+    prepares = [prepare(g) for g in range(GROUPS)]
+
+    def far_sums(g):
+        sums[g][0](4)
+        sums[g][1](3)
+
+    def near_sums(g):
+        sums[g][2](0, 4, 4)
+        sums[g][2](5, 9, 4)
+
+    lax.fori_loop(0, PLANES, arrived, 0)
+    far_sums(0)
+    rings(first, 0, "far")
+    near_sums(0)
+    rings(first, 0, "near")
+    slab_sums(0, x, y)
+    far_sums(1)
+    rings(first, 0, "relay")
+    rings(first, 1, "far")
+    near_sums(1)
+    slab_sums(1, x, y)
+    fetch_t.wait()
+    prepares[0](0, 16)
+    middle(0)
+    rings(first, 1, "near")
+    prepares[1](0, 16)
+    rings(first, 1, "relay")
+    for copy in late:
+        copy.wait()
+    fetch_weights.wait()
+    grid_begin(0)
+    grid_units(0, 0, 8)
+    middle(1)
+    grid_end(0)
     both(0, "begin")
-    if GROUPS == 2:
-        middle(1)
-        both(0, "pass_inner")
-        rings(second, 1, "relay")
-        both(0, "relay", 0)
-        grid(1)
-        both(1, "begin")
-    else:
-        both(0, "pass_inner")
-        both(0, "relay", 0)
+    both(0, "pass_inner")
+    both(0, "relay", 0)
+    grid_begin(1)
+    grid_units(1, 0, 4)
     both(0, "last_inner")
+    grid_units(1, 4, 8)
+    grid_end(1)
+    both(1, "begin")
     both(0, "relay", 1)
     both(0, "relay", 2)
-    if GROUPS == 2:
-        both(1, "pass_inner")
+    backs[0][2](0, 5, 5)
     both(0, "relay", 3)
-    for g in range(GROUPS):
-        far_back, near_back = over_slabs(functools.partial(slab_back, g))
-        if g == 1:
-            both(1, "last_inner")
-            both(1, "relay", 1)
-            both(1, "relay", 2)
-            both(1, "relay", 3)
-        near_back(0, 9, 3)
-        if g == 0 and GROUPS == 2:
-            both(1, "relay", 0)
-        both(g, "last")
-        far_back()
+    both(1, "pass_inner")
+    backs[0][2](5, 9, 4)
+    both(1, "relay", 0)
+    both(1, "last_inner")
+    for k in range(4):
+        both(0, "last", k)
+    backs[0][0](4)
+    both(1, "relay", 1)
+    both(1, "relay", 2)
+    backs[0][1](3)
+    backs[1][2](0, 5, 5)
+    both(1, "relay", 3)
+    backs[1][2](5, 9, 4)
+    for k, step in enumerate((0, 3, 1, 2)):
+        both(1, "last", k)
+        slab_back(1, up(x, 2), up(y, step))
+        if step != 2:
+            slab_back(1, up(x, step), up(y, 2))
 
     def slabs_arrived(p, carry):
         slab_pair(p).wait_recv()
@@ -591,14 +651,29 @@
                 term[1, i, half, every, :] = sens_re * field_im - sens_im * field_re
         for k in range(4):
             coil_copy(i, k).start()
-
-        @pl.when(i > 0)
-        def _():
-            coil_relay(i - 1)
-
-        return carry
-
-    lax.fori_loop(0, PLANES, plane_back, 0)
+        return carry
+
+    def plane_and_relay(i, carry):
+        plane_back(i, carry)
+        coil_relay(i - 2)
+        return carry
+
+    def sent(i, carry):
+        pair(i).wait_send()
+        slab_pair(2 * i).wait_send()
+        slab_pair(2 * i + 1).wait_send()
+        return carry
+
+    lax.fori_loop(0, 2, plane_back, 0)
+    for ring in first + second:
+        ring.drain()
+    for g in range(GROUPS):
+        both(g, "drain")
+    for copy in spread:
+        copy.wait_send()
+    lax.fori_loop(0, PLANES, sent, 0)
+    lax.fori_loop(2, PLANES, plane_and_relay, 0)
+    coil_relay(PLANES - 2)
     coil_relay(PLANES - 1)
 
     def store(i):
@@ -618,22 +693,10 @@
 
     def finished(i, carry):
         store(i).wait()
-        pair(i).wait_send()
-        return carry
-
-    def slabs_sent(p, carry):
-        slab_pair(p).wait_send()
         return carry
 
     lax.fori_loop(0, PLANES, collect, 0)
     lax.fori_loop(0, PLANES, finished, 0)
-    lax.fori_loop(0, CHIPS, slabs_sent, 0)
-    for ring in first + second:
-        ring.drain()
-    for g in range(GROUPS):
-        both(g, "drain")
-    for copy in spread:
-        copy.wait_send()
 
 
 def fused(image, sens, bins, live, weights, tab):
@@ -645,9 +708,15 @@
     return pl.pallas_call(
         kernel,
         out_shape=jax.ShapeDtypeStruct((2, PLANES, quarter, N), F32),
-        in_specs=[hbm, hbm, vmem, smem, hbm] + [vmem] * 6 + [hbm] * 2,
+        in_specs=[hbm, hbm, vmem, smem] + [hbm] * 9,
         out_specs=hbm,
         scratch_shapes=[
+            pltpu.VMEM((2, 3 * N, N), BF16),
+            pltpu.VMEM((2, N, 3 * N), BF16),
+            pltpu.VMEM((2, N, 3 * N), BF16),
+            pltpu.VMEM((2, 3 * N, N), BF16),
+            pltpu.VMEM((N, TILE), BF16),
+            pltpu.VMEM((TILE, N), BF16),
             pltpu.VMEM((2, PLANES, 2, N, TILE), F32),
             pltpu.VMEM((2, PLANES, 2, N, TILE), F32),
             pltpu.VMEM((SLOTS, TILE, TILE), BF16),
@@ -663,12 +732,10 @@
             pltpu.VMEM((rings, 2 * SPAN, TILE), F32),
             pltpu.VMEM((rings, 4 * SPAN, TILE), F32),
             pltpu.VMEM((rings, 4 * SPAN, TILE), F32),
-            pltpu.VMEM((rings, SPAN // 2, TILE), F32),
-            pltpu.VMEM((rings, SPAN // 2, TILE), F32),
-            pltpu.VMEM((rings, SPAN, TILE), F32),
-            pltpu.VMEM((rings, SPAN, TILE), F32),
+            pltpu.VMEM((rings, 3, SPAN, TILE), F32),
             pltpu.VMEM((4, SPAN, TILE), F32),
             pltpu.VMEM((2, SPAN, TILE), F32),
+            pltpu.VMEM((GROUPS, CHIPS, 4 * TILE, SPAN), BF16),
             pltpu.VMEM((GROUPS, RING, RING, SPAN, TILE), F32),
             pltpu.VMEM((GROUPS, RING, RING, SPAN, TILE), F32),
             pltpu.VMEM((3, CHIPS, PLANES, 2, 8, N), F32),
@@ -679,14 +746,16 @@
             pltpu.VMEM((2, PLANES, quarter, N), F32),
             pltpu.SemaphoreType.DMA((PLANES, 4)),
             pltpu.SemaphoreType.DMA,
-            pltpu.SemaphoreType.DMA((2,)),
+            pltpu.SemaphoreType.DMA((8,)),
             pltpu.SemaphoreType.DMA((PLANES,)),
             pltpu.SemaphoreType.DMA((CHIPS - 1,)),
             pltpu.SemaphoreType.DMA((CHIPS - 1,)),
             pltpu.SemaphoreType.DMA((PLANES,)),
             pltpu.SemaphoreType.DMA((PLANES,)),
-            pltpu.SemaphoreType.DMA((2 * rings, 6)),
-            pltpu.SemaphoreType.DMA((2 * rings, 6)),
+            pltpu.SemaphoreType.DMA((rings, 6)),
+            pltpu.SemaphoreType.DMA((rings, 6)),
+            pltpu.SemaphoreType.DMA((rings, 3)),
+            pltpu.SemaphoreType.DMA((rings, 3)),
             pltpu.SemaphoreType.DMA((rings, 20)),
             pltpu.SemaphoreType.DMA((rings, 20)),
             pltpu.SemaphoreType.DMA((CHIPS,)),

time: 135 us -> 120 us (0.89)
  Pallas kernels: 132 us -> 117 us
    pallas_call x1, Pallas kernels: 132 us -> 117 us  [fused(): pl.pallas_call(kernel, out_shape=jax.ShapeDtypeStruct((2, PLANES, quarter...]
where the time goes in v1:
time: 120 us; the launch traced here: 119 us
  Pallas kernels  117 us (98%)
  local copies, waits for them, and re-layouts  2.29 us (2%)
    pallas_call x1, Pallas kernels, fused(): pl.pallas_call(kernel, out_shape=jax.ShapeDtypeStruct((2, PLANES, quarter...  117 us

profile of v1, /device:TPU:1, one launch (start us, length us, event | category | flops | bytes accessed | tf_op | source)
XLA Modules:
  0.0 119.5 jit_solution(15329237256031832942)
XLA Ops:
  0.7 116.5 %shard_map.127 = f32[2,8,64,256]{3,2,1,0:T(8,128)} custom-call(f32[2,8,256,256]{3,2,1,0:T(8,128)} %image.1, f32[1,2,8,256,256]{4,3,2,1,0:T(8,128)} %sens.1, s32[1,256]{1,0:T(1,128)} %bitcast.1, s32[1]{0:T(128)S(6)} %copy.15.live, bf16[256,128,128]{2,1,0:T(8,128)(2,1)} %weights.1, bf16[2,768,256]{2,1,0:T(8,128)(2,1)} %constant.16.clone.fwd_right_hbm, ...), custom_call_target="tpu_custom_call" | custom-call | tf_op jit(solution)/shard_map/pallas_call | solution.py:708
  117.2 2.3 %copy.16 = f32[2,8,64,256]{3,2,1,0:T(8,128)} copy(f32[2,8,64,256]{3,2,1,0:T(8,128)} %shard_map.127) | data formatting | bytes 2097152

commit v2 on v1

--- a/solution.py
+++ b/solution.py
@@ -120,7 +120,7 @@
 
 def halved(source, target, sem, i, first):
     return [
-        pltpu.make_async_copy(source.at[:, i, :, pl.ds(half * TILE, TILE)], target.at[:, i, half], sem.at[i, first + half])
+        pltpu.make_async_copy(source.at[:, i, :, pl.ds(half * TILE, TILE)], target.at[:, i, half], sem.at[i, first])
         for half in range(2)
     ]
 
@@ -135,6 +135,10 @@
     return pltpu.make_async_remote_copy(
         src_ref=src, dst_ref=dst, send_sem=send, recv_sem=recv, device_id=peer, device_id_type=pl.DeviceIdType.MESH
     )
+
+
+def settle(ref, sem):
+    pltpu.make_async_copy(ref, ref, sem).wait()
 
 
 class RingSum:
@@ -145,13 +149,14 @@
         self.via_up, self.via_down, self.from_down, self.from_up = via_up, via_down, from_down, from_up
         first, second = self.half
         far, near_up, near_down = up(me, 2), up(me), down(me)
+        self.send, self.recv = send, recv
         self.copies = [
-            remote(src.at[far, first], via_up, send.at[0], recv.at[0], above),
-            remote(src.at[far, second], via_down, send.at[1], recv.at[1], below),
-            remote(src.at[near_up, second], from_down.at[second], send.at[2], recv.at[2], above),
-            remote(src.at[near_down, first], from_up.at[first], send.at[3], recv.at[3], below),
-            remote(src.at[near_up, first], from_down.at[first], send.at[4], recv.at[4], above),
-            remote(src.at[near_down, second], from_up.at[second], send.at[5], recv.at[5], below),
+            remote(src.at[far, first], via_up, send, recv.at[0], above),
+            remote(src.at[far, second], via_down, send, recv.at[1], below),
+            remote(src.at[near_up, second], from_down.at[second], send, recv.at[2], above),
+            remote(src.at[near_down, first], from_up.at[first], send, recv.at[2], below),
+            remote(src.at[near_up, first], from_down.at[first], send, recv.at[2], above),
+            remote(src.at[near_down, second], from_up.at[second], send, recv.at[2], below),
         ]
 
     def far(self):
@@ -174,22 +179,20 @@
         self.copies[5].start()
 
     def arrive(self):
-        for k in (2, 3, 4, 5):
-            self.copies[k].wait_recv()
+        settle(self.src.at[pl.ds(0, 2)], self.recv.at[2])
 
     def total(self, rows):
         return self.src[self.me, rows] + self.from_down[rows] + self.from_up[rows]
 
     def drain(self):
-        for copy in self.copies:
-            copy.wait_send()
+        settle(self.src.at[pl.ds(0, 3)], self.send)
 
 
 class RingDirect:
     def __init__(self, src, slots, send, recv, me, peers):
-        self.src, self.slots, self.me = src, slots, me
+        self.src, self.slots, self.me, self.send, self.recv = src, slots, me, send, recv
         self.copies = [
-            remote(src.at[up(me, step)], slots.at[k], send.at[k], recv.at[k], peer)
+            remote(src.at[up(me, step)], slots.at[k], send, recv, peer)
             for k, (step, peer) in enumerate(zip((2, 1, 3), peers))
         ]
 
@@ -198,15 +201,13 @@
             copy.start()
 
     def arrive(self):
-        for copy in self.copies:
-            copy.wait_recv()
+        settle(self.slots, self.recv)
 
     def total(self):
         return self.src[self.me] + self.slots[0] + self.slots[1] + self.slots[2]
 
     def drain(self):
-        for copy in self.copies:
-            copy.wait_send()
+        settle(self.slots, self.send)
 
 
 class PlaneGather:
@@ -215,51 +216,52 @@
         first, second = pl.ds(0, rows // 2), pl.ds(rows // 2, rows // 2)
         row, below, above = buf.at[outer], buf.at[down(outer)], buf.at[up(outer)]
 
-        def same(ref, k, peer):
-            return remote(ref, ref, send.at[k], recv.at[k], peer)
+        self.buf, self.send, self.recv = buf, send, recv
+
+        def same(ref, s, r, peer):
+            return remote(ref, ref, send.at[s], recv.at[r], peer)
 
         self.inner = [
-            same(row.at[inner], 0, inner_up),
-            same(row.at[inner], 1, inner_down),
-            same(row.at[down(inner), first], 2, inner_up),
-            same(row.at[up(inner), second], 3, inner_down),
+            same(row.at[inner], 0, 0, inner_up),
+            same(row.at[inner], 0, 0, inner_down),
+            same(row.at[down(inner), first], 0, 1, inner_up),
+            same(row.at[up(inner), second], 0, 1, inner_down),
         ]
         pieces = [inner, down(inner), up(inner), up(inner, 2)]
-        self.direct = [(same(row.at[p], 4 + 2 * k, outer_up), same(row.at[p], 5 + 2 * k, outer_down)) for k, p in enumerate(pieces)]
+        self.direct = [(same(row.at[p], 1, 2 + k, outer_up), same(row.at[p], 1, 2 + k, outer_down)) for k, p in enumerate(pieces)]
         self.relays = [
-            (same(below.at[p, first], 12 + 2 * k, outer_up), same(above.at[p, second], 13 + 2 * k, outer_down))
+            (same(below.at[p, first], 1, 6 + k, outer_up), same(above.at[p, second], 1, 6 + k, outer_down))
             for k, p in enumerate(pieces)
         ]
+
+    def some(self, pieces):
+        return self.buf.at[0, pl.ds(0, pieces)]
 
     def begin(self):
         for copy in self.inner[:2] + list(self.direct[0]):
             copy.start()
 
     def pass_inner(self):
-        for k in range(2):
-            self.inner[k].wait_recv()
-            self.inner[2 + k].start()
-            for copy in self.direct[1 + k]:
-                copy.start()
+        settle(self.some(2), self.recv.at[0])
+        for copy in self.inner[2:] + list(self.direct[1] + self.direct[2]):
+            copy.start()
 
     def last_inner(self):
-        for k in (2, 3):
-            self.inner[k].wait_recv()
+        settle(self.some(1), self.recv.at[1])
         for copy in self.direct[3]:
             copy.start()
 
     def relay(self, piece):
-        for k in range(2):
-            self.direct[piece][k].wait_recv()
-            self.relays[piece][k].start()
+        settle(self.some(2), self.recv.at[2 + piece])
+        for copy in self.relays[piece]:
+            copy.start()
 
     def last(self, piece):
-        for copy in self.relays[piece]:
-            copy.wait_recv()
+        settle(self.some(1), self.recv.at[6 + piece])
 
     def drain(self):
-        for copy in self.inner + [copy for pair in self.direct + self.relays for copy in pair]:
-            copy.wait_send()
+        settle(self.some(3), self.send.at[0])
+        settle(self.buf.at[pl.ds(0, 3)], self.send.at[1])
 
 
 def kernel(
@@ -279,7 +281,7 @@
     others = [{"slab": lax.rem(chip + k, CHIPS) * 2 + core} for k in range(1, CHIPS)]
     peers = [sibling, over, under] + others
     def loads(i):
-        return halved(image, image_buf, load_sem, i, 0) + halved(sens.at[0], sens_buf, load_sem, i, 2)
+        return halved(image, image_buf, load_sem, i, 0) + halved(sens.at[0], sens_buf, load_sem, i, 1)
 
     def start_load(i, carry):
         for copy in loads(i):
@@ -303,14 +305,14 @@
     lax.fori_loop(1, PLANES, start_load, 0)
     fetch.start()
     bins_row[chip] = jnp.broadcast_to(bins[...].astype(F32), (8, SLOTS))
-    spread = [remote(bins_row.at[chip], bins_row.at[chip], bin_send.at[k], bin_recv.at[k], others[k]) for k in range(CHIPS - 1)]
+    spread = [remote(bins_row.at[chip], bins_row.at[chip], bin_send, bin_recv, others[k]) for k in range(CHIPS - 1)]
 
     def pair(i):
-        return remote(field.at[2, i], field.at[core, i], pair_send.at[i], pair_recv.at[i], sibling)
+        return remote(field.at[2, i], field.at[core, i], pair_send, pair_recv, sibling)
 
     def plane_forward(i):
-        for copy in loads(i):
-            copy.wait()
+        settle(image_buf.at[:, i], load_sem.at[i, 0])
+        settle(sens_buf.at[:, i], load_sem.at[i, 1])
         summed, differed = [], []
         for odd in range(2):
             rows = pl.ds(odd, TILE, stride=2)
@@ -358,8 +360,7 @@
     for copy in late:
         copy.start()
     fetch.wait()
-    for copy in spread:
-        copy.wait_recv()
+    settle(bins_row.at[pl.ds(0, CHIPS - 1)], bin_recv)
     bins_col[...] = bins_row[...].reshape(CHIPS * 8, SLOTS).T
     lane = lax.broadcasted_iota(jnp.int32, (SPAN, TILE), 1)
 
@@ -485,7 +486,7 @@
         all_b[g, y, x] = back[SPAN:]
 
     def slab_pair(p):
-        return remote(planes_back.at[2, p], planes_back.at[core, p], slab_send.at[p], slab_recv.at[p], sibling)
+        return remote(planes_back.at[2, p], planes_back.at[core, p], slab_send, slab_recv, sibling)
 
     def prepare(g):
         def one(p, carry):
@@ -522,10 +523,6 @@
         if g == GROUPS - 1:
             slab_pair(p).start()
 
-    def arrived(i, carry):
-        pair(i).wait_recv()
-        return carry
-
     def both(g, action, *args):
         for gather in gathers[g]:
             getattr(gather, action)(*args)
@@ -542,7 +539,7 @@
         sums[g][2](0, 4, 4)
         sums[g][2](5, 9, 4)
 
-    lax.fori_loop(0, PLANES, arrived, 0)
+    settle(field.at[2], pair_recv)
     far_sums(0)
     rings(first, 0, "far")
     near_sums(0)
@@ -598,11 +595,7 @@
         if step != 2:
             slab_back(1, up(x, step), up(y, 2))
 
-    def slabs_arrived(p, carry):
-        slab_pair(p).wait_recv()
-        return carry
-
-    lax.fori_loop(0, CHIPS, slabs_arrived, 0)
+    settle(planes_back.at[2], slab_recv)
 
     term = image_buf
     quarter = N // RING
@@ -620,7 +613,7 @@
             (share(0, i, near_up), from_down.at[i, 0], over),
             (share(1, i, near_down), from_up.at[i, 1], under),
         )[k]
-        return remote(source, target, coil_send.at[i, k], coil_recv.at[i, k], peer)
+        return remote(source, target, coil_send.at[k // 4], coil_recv.at[i, min(k, 2)], peer)
 
     def coil_relay(i):
         coil_copy(i, 0).wait_recv()
@@ -658,45 +651,34 @@
         coil_relay(i - 2)
         return carry
 
-    def sent(i, carry):
-        pair(i).wait_send()
-        slab_pair(2 * i).wait_send()
-        slab_pair(2 * i + 1).wait_send()
-        return carry
-
     lax.fori_loop(0, 2, plane_back, 0)
     for ring in first + second:
         ring.drain()
     for g in range(GROUPS):
         both(g, "drain")
-    for copy in spread:
-        copy.wait_send()
-    lax.fori_loop(0, PLANES, sent, 0)
+    settle(bins_row.at[pl.ds(0, CHIPS - 1)], bin_send)
+    settle(field.at[2], pair_send)
+    settle(planes_back.at[2], slab_send)
     lax.fori_loop(2, PLANES, plane_and_relay, 0)
     coil_relay(PLANES - 2)
     coil_relay(PLANES - 1)
 
     def store(i):
-        return pltpu.make_async_copy(result.at[:, i], out.at[:, i], out_sem.at[i])
+        return pltpu.make_async_copy(result.at[:, i], out.at[:, i], out_sem)
 
     def collect(i, carry):
-        for k in (2, 3, 4, 5):
-            coil_copy(i, k).wait_recv()
+        settle(from_down.at[pl.ds(0, 2)], coil_recv.at[i, 2])
         for part in range(2):
             total = share(part, i, coil)[...] + from_down[i, part] + from_up[i, part]
             for half in range(2):
                 result[part, i, :, half * TILE : (half + 1) * TILE] = total[half]
         store(i).start()
-        for k in range(6):
-            coil_copy(i, k).wait_send()
         return carry
 
-    def finished(i, carry):
-        store(i).wait()
-        return carry
-
     lax.fori_loop(0, PLANES, collect, 0)
-    lax.fori_loop(0, PLANES, finished, 0)
+    settle(field.at[2], coil_send.at[0])
+    settle(from_down, coil_send.at[1])
+    settle(result, out_sem)
 
 
 def fused(image, sens, bins, live, weights, tab):
@@ -744,24 +726,24 @@
             pltpu.VMEM((PLANES, 2, 2, quarter, TILE), F32),
             pltpu.VMEM((PLANES, 2, 2, quarter, TILE), F32),
             pltpu.VMEM((2, PLANES, quarter, N), F32),
-            pltpu.SemaphoreType.DMA((PLANES, 4)),
+            pltpu.SemaphoreType.DMA((PLANES, 2)),
             pltpu.SemaphoreType.DMA,
             pltpu.SemaphoreType.DMA((8,)),
-            pltpu.SemaphoreType.DMA((PLANES,)),
-            pltpu.SemaphoreType.DMA((CHIPS - 1,)),
-            pltpu.SemaphoreType.DMA((CHIPS - 1,)),
-            pltpu.SemaphoreType.DMA((PLANES,)),
-            pltpu.SemaphoreType.DMA((PLANES,)),
-            pltpu.SemaphoreType.DMA((rings, 6)),
-            pltpu.SemaphoreType.DMA((rings, 6)),
+            pltpu.SemaphoreType.DMA,
+            pltpu.SemaphoreType.DMA,
+            pltpu.SemaphoreType.DMA,
+            pltpu.SemaphoreType.DMA,
+            pltpu.SemaphoreType.DMA,
+            pltpu.SemaphoreType.DMA((rings,)),
             pltpu.SemaphoreType.DMA((rings, 3)),
-            pltpu.SemaphoreType.DMA((rings, 3)),
-            pltpu.SemaphoreType.DMA((rings, 20)),
-            pltpu.SemaphoreType.DMA((rings, 20)),
-            pltpu.SemaphoreType.DMA((CHIPS,)),
-            pltpu.SemaphoreType.DMA((CHIPS,)),
-            pltpu.SemaphoreType.DMA((PLANES, 6)),
-            pltpu.SemaphoreType.DMA((PLANES, 6)),
+            pltpu.SemaphoreType.DMA((rings,)),
+            pltpu.SemaphoreType.DMA((rings,)),
+            pltpu.SemaphoreType.DMA((rings, 2)),
+            pltpu.SemaphoreType.DMA((rings, 10)),
+            pltpu.SemaphoreType.DMA,
+            pltpu.SemaphoreType.DMA,
+            pltpu.SemaphoreType.DMA((2,)),
+            pltpu.SemaphoreType.DMA((PLANES, 3)),
         ],
         compiler_params=pltpu.CompilerParams(collective_id=0, has_side_effects=True, vmem_limit_bytes=VMEM_LIMIT),
     )(

time: 120 us -> 117 us (0.975)
  Pallas kernels: 117 us -> 114 us
    pallas_call x1, Pallas kernels: 117 us -> 114 us  [fused(): pl.pallas_call(kernel, out_shape=jax.ShapeDtypeStruct((2, PLANES, quarter...]
where the time goes in v2:
time: 117 us
  Pallas kernels  114 us (97%)
  local copies, waits for them, and re-layouts  2.29 us (2%)
    pallas_call x1, Pallas kernels, fused(): pl.pallas_call(kernel, out_shape=jax.ShapeDtypeStruct((2, PLANES, quarter...  114 us

profile of v2, /device:TPU:1, one launch (start us, length us, event | category | flops | bytes accessed | tf_op | source)
XLA Modules:
  0.0 116.9 jit_solution(8393784990246768904)
XLA Ops:
  0.7 113.9 %shard_map.127 = f32[2,8,64,256]{3,2,1,0:T(8,128)} custom-call(f32[2,8,256,256]{3,2,1,0:T(8,128)} %image.1, f32[1,2,8,256,256]{4,3,2,1,0:T(8,128)} %sens.1, s32[1,256]{1,0:T(1,128)} %bitcast.1, s32[1]{0:T(128)S(6)} %copy.15.live, bf16[256,128,128]{2,1,0:T(8,128)(2,1)} %weights.1, bf16[2,768,256]{2,1,0:T(8,128)(2,1)} %constant.16.clone.fwd_right_hbm, ...), custom_call_target="tpu_custom_call" | custom-call | tf_op jit(solution)/shard_map/pallas_call | solution.py:690
  114.6 2.3 %copy.16 = f32[2,8,64,256]{3,2,1,0:T(8,128)} copy(f32[2,8,64,256]{3,2,1,0:T(8,128)} %shard_map.127) | data formatting | bytes 2097152

commit v3 on v2

--- a/solution.py
+++ b/solution.py
@@ -152,11 +152,11 @@
         self.send, self.recv = send, recv
         self.copies = [
             remote(src.at[far, first], via_up, send, recv.at[0], above),
-            remote(src.at[far, second], via_down, send, recv.at[1], below),
-            remote(src.at[near_up, second], from_down.at[second], send, recv.at[2], above),
-            remote(src.at[near_down, first], from_up.at[first], send, recv.at[2], below),
-            remote(src.at[near_up, first], from_down.at[first], send, recv.at[2], above),
-            remote(src.at[near_down, second], from_up.at[second], send, recv.at[2], below),
+            remote(src.at[far, second], via_down, send, recv.at[0], below),
+            remote(src.at[near_up, second], from_down.at[second], send, recv.at[1], above),
+            remote(src.at[near_down, first], from_up.at[first], send, recv.at[1], below),
+            remote(src.at[near_up, first], from_down.at[first], send, recv.at[1], above),
+            remote(src.at[near_down, second], from_up.at[second], send, recv.at[1], below),
         ]
 
     def far(self):
@@ -169,17 +169,16 @@
 
     def relay(self):
         first, second = self.half
-        self.copies[0].wait_recv()
+        settle(self.src.at[0], self.recv.at[0])
         near = up(self.me)
         self.src[near, first] = self.src[near, first] + self.via_up[...]
         self.copies[4].start()
-        self.copies[1].wait_recv()
         near = down(self.me)
         self.src[near, second] = self.src[near, second] + self.via_down[...]
         self.copies[5].start()
 
     def arrive(self):
-        settle(self.src.at[pl.ds(0, 2)], self.recv.at[2])
+        settle(self.src.at[pl.ds(0, 2)], self.recv.at[1])
 
     def total(self, rows):
         return self.src[self.me, rows] + self.from_down[rows] + self.from_up[rows]
@@ -533,6 +532,8 @@
 
     def far_sums(g):
         sums[g][0](4)
+        if g == 0:
+            first[0].far()
         sums[g][1](3)
 
     def near_sums(g):
@@ -541,7 +542,7 @@
 
     settle(field.at[2], pair_recv)
     far_sums(0)
-    rings(first, 0, "far")
+    first[1].far()
     near_sums(0)
     rings(first, 0, "near")
     slab_sums(0, x, y)
@@ -613,14 +614,13 @@
             (share(0, i, near_up), from_down.at[i, 0], over),
             (share(1, i, near_down), from_up.at[i, 1], under),
         )[k]
-        return remote(source, target, coil_send.at[k // 4], coil_recv.at[i, min(k, 2)], peer)
+        return remote(source, target, coil_send.at[k // 4], coil_recv.at[i, min(k // 2, 1)], peer)
 
     def coil_relay(i):
-        coil_copy(i, 0).wait_recv()
+        settle(from_down.at[0], coil_recv.at[i, 0])
         ref = share(0, i, near_up)
         ref[...] = ref[...] + via_up[i]
         coil_copy(i, 4).start()
-        coil_copy(i, 1).wait_recv()
         ref = share(1, i, near_down)
         ref[...] = ref[...] + via_down[i]
         coil_copy(i, 5).start()
@@ -667,7 +667,7 @@
         return pltpu.make_async_copy(result.at[:, i], out.at[:, i], out_sem)
 
     def collect(i, carry):
-        settle(from_down.at[pl.ds(0, 2)], coil_recv.at[i, 2])
+        settle(from_down.at[pl.ds(0, 2)], coil_recv.at[i, 1])
         for part in range(2):
             total = share(part, i, coil)[...] + from_down[i, part] + from_up[i, part]
             for half in range(2):
@@ -735,7 +735,7 @@
             pltpu.SemaphoreType.DMA,
             pltpu.SemaphoreType.DMA,
             pltpu.SemaphoreType.DMA((rings,)),
-            pltpu.SemaphoreType.DMA((rings, 3)),
+            pltpu.SemaphoreType.DMA((rings, 2)),
             pltpu.SemaphoreType.DMA((rings,)),
             pltpu.SemaphoreType.DMA((rings,)),
             pltpu.SemaphoreType.DMA((rings, 2)),
@@ -743,7 +743,7 @@
             pltpu.SemaphoreType.DMA,
             pltpu.SemaphoreType.DMA,
             pltpu.SemaphoreType.DMA((2,)),
-            pltpu.SemaphoreType.DMA((PLANES, 3)),
+            pltpu.SemaphoreType.DMA((PLANES, 2)),
         ],
         compiler_params=pltpu.CompilerParams(collective_id=0, has_side_effects=True, vmem_limit_bytes=VMEM_LIMIT),
     )(

time: 117 us -> 117 us (level)
  no operation moved by 1% of the time
where the time goes in v3:
time: 117 us
  Pallas kernels  114 us (97%)
  local copies, waits for them, and re-layouts  2.29 us (2%)
    pallas_call x1, Pallas kernels, fused(): pl.pallas_call(kernel, out_shape=jax.ShapeDtypeStruct((2, PLANES, quarter...  114 us

profile of v3, /device:TPU:1, one launch (start us, length us, event | category | flops | bytes accessed | tf_op | source)
XLA Modules:
  0.0 116.6 jit_solution(491178889444259658)
XLA Ops:
  0.7 113.7 %shard_map.127 = f32[2,8,64,256]{3,2,1,0:T(8,128)} custom-call(f32[2,8,256,256]{3,2,1,0:T(8,128)} %image.1, f32[1,2,8,256,256]{4,3,2,1,0:T(8,128)} %sens.1, s32[1,256]{1,0:T(1,128)} %bitcast.1, s32[1]{0:T(128)S(6)} %copy.15.live, bf16[256,128,128]{2,1,0:T(8,128)(2,1)} %weights.1, bf16[2,768,256]{2,1,0:T(8,128)(2,1)} %constant.16.clone.fwd_right_hbm, ...), custom_call_target="tpu_custom_call" | custom-call | tf_op jit(solution)/shard_map/pallas_call | solution.py:690
  114.3 2.3 %copy.16 = f32[2,8,64,256]{3,2,1,0:T(8,128)} copy(f32[2,8,64,256]{3,2,1,0:T(8,128)} %shard_map.127) | data formatting | bytes 2097152
